TPU v7x, 128 devices: a whole 4x4x4 slice. The times are simulated.
128 devices in a mesh: section: 16 (over y_hi, x, core), ctx: 8 (over y_lo, z).
Axes of the slice: x: 4, y: 4 (y_hi: 2, y_lo: 2; y = y_hi * 2 + y_lo), z: 4, core: 2. Of those that a mesh axis runs over, the one named last changes fastest.
Arguments:
- section_input: bfloat16 [16, 2048, 5120], P('section', 'ctx'), may hold values from -60 to 60
- last_hidden: bfloat16 [2048, 5120], P('section'), may hold values from -60 to 60
- kv_gain: float32 [5120], replicated, may hold values from 0.25 to 1.75
- query_gain: float32 [16, 5120], P('section'), may hold values from 0.25 to 1.75
- w_key: bfloat16 [5120, 3072], P(None, 'ctx'), may hold values from -1 to 1
- w_value: bfloat16 [5120, 3072], P(None, 'ctx'), may hold values from -0.078125 to 0.078125
- w_query: bfloat16 [16, 5120, 3072], P('section', None, 'ctx'), may hold values from -30 to 30
- w_out: bfloat16 [16, 3072, 5120], P('section', None, 'ctx'), may hold values from -0.625 to 0.625
- segment_ids: int32 [2048], replicated, may hold values from 0 to 3, never falling along the last dimension, each value on 1 to 1024 neighbouring positions
Outputs:
- layer_output: bfloat16 [16, 2048, 5120], P('section', None, 'ctx')
Inputs may be any that keep to these rules, and one draw needn't show every extreme that they name: `segment_ids`: documents are runs of equal ids that never fall; the longest holds exactly 1024 tokens.
All inputs are finite; a program needn't handle non-finite values.
Results may differ from a plain program's by a relative error of at most 0.005.
The roundings to bfloat16 on the way count: a program that leaves them out, or rounds other values in their place, can miss the bound.
Values may be sent and summed in bfloat16 or wider, within the bound.
No kernel may reach another device: no remote copies, remote signals or barrier semaphores. Data moves between devices by JAX's collectives and lax.ppermute only.
A program may use at most 128 MiB of HBM per device.

v0:
```python
import math
import jax
import jax.numpy as jnp
from jax import lax
from jax.sharding import PartitionSpec as P

HD = 128


def normalize(rows, gain):
    full = rows.astype(jnp.float32)
    scaled = full * lax.rsqrt(jnp.mean(full * full, axis=-1, keepdims=True) + 1e-05) * gain
    return scaled.astype(jnp.bfloat16)


def body(
    section_input, last_hidden, kv_gain, query_gain, w_key, w_value, w_query, w_out, segment_ids
):
    layer_rows = section_input[0]
    gain = query_gain[0]
    w_q = w_query[0]
    w_o = w_out[0]
    width = w_o.shape[1]
    head_cols = w_q.shape[1]
    first_col = lax.axis_index("ctx") * width
    kv_in = normalize(last_hidden, kv_gain)
    own_keys = jnp.dot(kv_in, w_key, preferred_element_type=jnp.float32).astype(jnp.bfloat16)
    own_values = jnp.dot(kv_in, w_value, preferred_element_type=jnp.float32).astype(jnp.bfloat16)
    keys, values = (
        lax.all_gather(own_keys, "section", axis=0, tiled=True),
        lax.all_gather(own_values, "section", axis=0, tiled=True),
    )
    piece = lax.all_gather(layer_rows, "ctx", axis=0, tiled=True)
    queries_part = jnp.dot(normalize(piece, gain), w_q, preferred_element_type=jnp.float32).astype(
        jnp.bfloat16
    )
    features = lax.dynamic_slice_in_dim(piece, first_col, width, 1)
    joined = jnp.concatenate([queries_part, features], axis=1)
    queries = joined[:, :head_cols]
    residual = joined[:, head_cols:]
    total_rows = queries.shape[0]
    local_heads = head_cols // HD
    block = math.gcd(total_rows, 512)
    key_heads = keys.reshape(total_rows, local_heads, HD)
    value_heads = values.reshape(total_rows, local_heads, HD)
    places = jnp.arange(total_rows, dtype=jnp.int32)
    scale = HD ** (-0.5)

    def attend(start):
        rows = lax.dynamic_slice_in_dim(queries, start, block, 0).reshape(block, local_heads, HD)
        scores = (
            jnp.einsum("qhd,khd->hqk", rows, key_heads, preferred_element_type=jnp.float32) * scale
        )
        query_places = start + jnp.arange(block, dtype=jnp.int32)
        query_docs = lax.dynamic_slice_in_dim(segment_ids, start, block, 0)
        visible = (places[None, :] <= query_places[:, None]) & (
            segment_ids[None, :] == query_docs[:, None]
        )
        scores = jnp.where(visible[None], scores, -1e30)
        top = jnp.max(scores, axis=-1, keepdims=True)
        expo = jnp.where(visible[None], jnp.exp(scores - top), 0.0)
        weights = (expo / jnp.sum(expo, axis=-1, keepdims=True)).astype(jnp.bfloat16)
        mixed = jnp.einsum("hqk,khd->qhd", weights, value_heads, preferred_element_type=jnp.float32)
        return mixed.reshape(block, head_cols).astype(jnp.bfloat16)

    starts = jnp.arange(total_rows // block, dtype=jnp.int32) * block
    context = lax.map(attend, starts).reshape(total_rows, head_cols)
    summed = jnp.dot(
        lax.all_gather(context, "ctx", axis=1, tiled=True), w_o, preferred_element_type=jnp.float32
    )
    result = (residual.astype(jnp.float32) + summed).astype(jnp.bfloat16)
    return result[None]


def solution(mesh):
    return jax.shard_map(
        body,
        mesh=mesh,
        in_specs=(
            P("section", "ctx", None),
            P("section", None),
            P(),
            P("section", None),
            P(None, "ctx"),
            P(None, "ctx"),
            P("section", None, "ctx"),
            P("section", None, "ctx"),
            P(),
        ),
        out_specs=P("section", None, "ctx"),
        check_vma=False,
    )
```

profile of v0, /device:TPU:1, one launch (start us, length us, event | category | flops | bytes accessed | tf_op | source)
XLA Modules:
  0.0 596.5 jit_solution(7061110203736118931)
XLA Ops:
  6.5 1.8 fusion.36
  8.3 4.1 convolution_convert_fusion.1
  12.5 3.6 convolution_convert_fusion
  16.2 0.7 all-gather.12.cloned.1.call-update
  17.0 45.9 %all-gather.6.cloned.1.call-done = bf16[2048,384]{1,0:T(8,128)(2,1)} async-done(((bf16[128,384]{1,0:T(8,128)(2,1)}), bf16[2048,384]{1,0:T(8,128)(2,1)}) %all-gather.6.cloned.1.call-update) | async-done | bytes 1572880 | tf_op jit(solution)/shard_map/all_gather | solution.py:30
  62.9 1.7 copy.13
  64.6 1.6 copy.16
  66.2 44.6 %all-gather.8.cloned.1.call-done = bf16[2048,384]{1,0:T(8,128)(2,1)} async-done(((bf16[128,384]{1,0:T(8,128)(2,1)}), bf16[2048,384]{1,0:T(8,128)(2,1)}) %all-gather.8.cloned.1.call-update) | async-done | bytes 1572880 | tf_op jit(solution)/shard_map/all_gather | solution.py:31
  110.8 2.6 copy.14
  113.5 207.5 %all-gather.12.cloned.1.call-done = bf16[1,2048,5120]{2,1,0:T(8,128)(2,1)} async-done(((bf16[1,256,5120]{2,1,0:T(8,128)(2,1)}), bf16[1,2048,5120]{2,1,0:T(8,128)(2,1)}) %all-gather.12.cloned.1.call-update) | async-done | bytes 20971536 | tf_op jit(solution)/shard_map/all_gather | solution.py:33
  321.0 9.1 %fusion.14 = f32[2048]{0:T(1024)S(1)} fusion(bf16[1,2048,5120]{2,1,0:T(8,128)(2,1)} %all-gather.12.cloned.1.call-done), kind=kLoop, calls=%fused_computation.21 | loop fusion | flops 31455232 | bytes 20979712 | tf_op jit(solution)/shard_map/reduce_sum | solution.py:12
  330.2 15.3 %fusion.31 = bf16[2048,384]{1,0:T(8,128)(2,1)S(1)} fusion(bf16[1,5120,384]{2,1,0:T(8,128)(2,1)S(1)} %copy-done.2, bf16[1,2048,5120]{2,1,0:T(8,128)(2,1)} %all-gather.12.cloned.1.call-done, f32[5120]{0:T(1024)S(1)} %bitcast.60, f32[2048]{0:T(1024)S(1)} %add_rsqrt_fusion), kind=kOutput, calls=%fused_computation.36 | convolution fusion | flops 8095793152 | bytes 26505216 | tf_op jit(solution)/shard_map/dot_general | solution.py:34
  345.5 98.6 %while.11 = (s32[]{:T(128)}, bf16[4,512,384]{2,1,0:T(8,128)(2,1)}, s32[4]{0:T(128)S(1)}, s32[2048]{0:T(1024)S(1)}, bf16[2048,384]{1,0:T(8,128)(2,1)S(1)}, /*inde...) while((s32[]{:T(128)}, bf16[4,512,384]{2,1,0:T(8,128)(2,1)}, ...), condition=%wide.region_5.6_spmd.clone, body=%wide.region_2.5_spmd.clone.sunk | while | flops 1635977728 | bytes 34372256 | solution.py:67
  348.8 1.0 fusion.59
  350.2 11.8 %fusion.60 = (f32[3,512]{1,0:T(4,128)S(1)}, f32[3,512,2048]{2,1,0:T(8,128)}) fusion(pred[512,2048]{1,0:T(8,128)(4,1)S(1)} %fusion.59, bf16[512,3,128]{0,2,1:T(8,128)(2,1)S(1)} %bitcast.55, bf16[2048,3,128]{2,0,1:T(8,128)(2,1)} %get-tuple-element.166), kind=kOutput, calls=%fused_computation.45.clone.1 | convolution fusion | flops 821037056 | bytes 15603712 | tf_op jit(solution)/shard_map/while/body/eval_jaxpr/sub | solution.py:61
  362.0 7.3 %fusion.61 = bf16[3,512,128]{1,2,0:T(8,128)(2,1)S(1)} fusion(bf16[2048,3,128]{0,2,1:T(8,128)(2,1)} %get-tuple-element.167, f32[3,512,2048]{2,1,0:T(8,128)} %get-tuple-element.139, f32[3,512]{1,0:T(4,128)S(1)} %get-tuple-element.140), kind=kOutput, calls=%fused_computation.13.clone.1 | convolution fusion | flops 811794432 | bytes 14555136 | tf_op jit(solution)/shard_map/while/body/eval_jaxpr/hqk,khd->qhd/dot_general | solution.py:63
  369.5 0.8 constant_dynamic-update-slice_fusion.2
  372.8 0.6 iota_add_fusion.2
  373.4 1.0 fusion.59
  374.8 11.8 %fusion.60 = (f32[3,512]{1,0:T(4,128)S(1)}, f32[3,512,2048]{2,1,0:T(8,128)}) fusion(pred[512,2048]{1,0:T(8,128)(4,1)S(1)} %fusion.59, bf16[512,3,128]{0,2,1:T(8,128)(2,1)S(1)} %bitcast.55, bf16[2048,3,128]{2,0,1:T(8,128)(2,1)} %get-tuple-element.166), kind=kOutput, calls=%fused_computation.45.clone.1 | convolution fusion | flops 821037056 | bytes 15603712 | tf_op jit(solution)/shard_map/while/body/eval_jaxpr/sub | solution.py:61
  386.6 7.3 %fusion.61 = bf16[3,512,128]{1,2,0:T(8,128)(2,1)S(1)} fusion(bf16[2048,3,128]{0,2,1:T(8,128)(2,1)} %get-tuple-element.167, f32[3,512,2048]{2,1,0:T(8,128)} %get-tuple-element.139, f32[3,512]{1,0:T(4,128)S(1)} %get-tuple-element.140), kind=kOutput, calls=%fused_computation.13.clone.1 | convolution fusion | flops 811794432 | bytes 14555136 | tf_op jit(solution)/shard_map/while/body/eval_jaxpr/hqk,khd->qhd/dot_general | solution.py:63
  394.1 0.8 constant_dynamic-update-slice_fusion.2
  398.1 1.0 fusion.59
  399.4 11.8 %fusion.60 = (f32[3,512]{1,0:T(4,128)S(1)}, f32[3,512,2048]{2,1,0:T(8,128)}) fusion(pred[512,2048]{1,0:T(8,128)(4,1)S(1)} %fusion.59, bf16[512,3,128]{0,2,1:T(8,128)(2,1)S(1)} %bitcast.55, bf16[2048,3,128]{2,0,1:T(8,128)(2,1)} %get-tuple-element.166), kind=kOutput, calls=%fused_computation.45.clone.1 | convolution fusion | flops 821037056 | bytes 15603712 | tf_op jit(solution)/shard_map/while/body/eval_jaxpr/sub | solution.py:61
  411.2 7.3 %fusion.61 = bf16[3,512,128]{1,2,0:T(8,128)(2,1)S(1)} fusion(bf16[2048,3,128]{0,2,1:T(8,128)(2,1)} %get-tuple-element.167, f32[3,512,2048]{2,1,0:T(8,128)} %get-tuple-element.139, f32[3,512]{1,0:T(4,128)S(1)} %get-tuple-element.140), kind=kOutput, calls=%fused_computation.13.clone.1 | convolution fusion | flops 811794432 | bytes 14555136 | tf_op jit(solution)/shard_map/while/body/eval_jaxpr/hqk,khd->qhd/dot_general | solution.py:63
  418.7 0.8 constant_dynamic-update-slice_fusion.2
  422.7 1.0 fusion.59
  424.0 11.8 %fusion.60 = (f32[3,512]{1,0:T(4,128)S(1)}, f32[3,512,2048]{2,1,0:T(8,128)}) fusion(pred[512,2048]{1,0:T(8,128)(4,1)S(1)} %fusion.59, bf16[512,3,128]{0,2,1:T(8,128)(2,1)S(1)} %bitcast.55, bf16[2048,3,128]{2,0,1:T(8,128)(2,1)} %get-tuple-element.166), kind=kOutput, calls=%fused_computation.45.clone.1 | convolution fusion | flops 821037056 | bytes 15603712 | tf_op jit(solution)/shard_map/while/body/eval_jaxpr/sub | solution.py:61
  435.8 7.3 %fusion.61 = bf16[3,512,128]{1,2,0:T(8,128)(2,1)S(1)} fusion(bf16[2048,3,128]{0,2,1:T(8,128)(2,1)} %get-tuple-element.167, f32[3,512,2048]{2,1,0:T(8,128)} %get-tuple-element.139, f32[3,512]{1,0:T(4,128)S(1)} %get-tuple-element.140), kind=kOutput, calls=%fused_computation.13.clone.1 | convolution fusion | flops 811794432 | bytes 14555136 | tf_op jit(solution)/shard_map/while/body/eval_jaxpr/hqk,khd->qhd/dot_general | solution.py:63
  443.3 0.8 constant_dynamic-update-slice_fusion.2
  444.2 130.2 %all-gather.10.cloned.1.call-done = bf16[2048,3072]{1,0:T(8,128)(2,1)} async-done(((bf16[2048,384]{1,0:T(8,128)(2,1)}), bf16[2048,3072]{1,0:T(8,128)(2,1)}) %all-gather.10.cloned.1.call-update) | async-done | bytes 12582928 | tf_op jit(solution)/shard_map/all_gather | solution.py:69
  574.4 15.5 %fusion.28 = bf16[1,2048,640]{2,1,0:T(8,128)(2,1)} fusion(bf16[2048,3072]{1,0:T(8,128)(2,1)} %all-gather.10.cloned.1.call-done, bf16[1,3072,640]{2,1,0:T(8,128)(2,1)} %param.18, bf16[1,2048,5120]{2,1,0:T(8,128)(2,1)} %all-gather.12.cloned.1.call-done, s32[]{:T(128)S(6)} %select_n.14), kind=kOutput, calls=%fused_computation.35 | convolution fusion | flops 8056995840 | bytes 21757956 | tf_op jit(solution)/shard_map/dot_general | solution.py:68
  (44 shorter events, 6.8 us)
Async XLA Ops:
  6.5 5.9 copy-start
  6.5 5.9 copy-start.3
  6.5 56.3 %all-gather.6.cloned.1.call-start = ((), (), s32[]{:S(2)}) async-start(), calls=%async_computation | async-start | bytes 1671168 | tf_op jit(solution)/shard_map/all_gather | solution.py:30
  12.4 98.4 %all-gather.8.cloned.1.call-start = ((), (), s32[]{:S(2)}) async-start(), calls=%async_computation.1 | async-start | bytes 1671168 | tf_op jit(solution)/shard_map/all_gather | solution.py:31
  16.1 304.8 %all-gather.12.cloned.1.call-start = ((), (), s32[]{:S(2)}) async-start(), calls=%async_computation.3 | async-start | bytes 23592960 | tf_op jit(solution)/shard_map/all_gather | solution.py:33
  16.9 557.5 %all-gather.10.cloned.1.call-start = ((), (), s32[]{:S(2)}) async-start(), calls=%async_computation.2 | async-start | bytes 14155776 | tf_op jit(solution)/shard_map/all_gather | solution.py:69
  113.5 216.7 %copy-start.4 = (f32[1,5120]{1,0:T(1,128)S(1)}, f32[1,5120]{1,0:T(1,128)}, u32[]{:S(2)}) copy-start(f32[1,5120]{1,0:T(1,128)} %param.14) | copy-start | bytes 61444
  321.0 9.2 %copy-start.2 = (bf16[1,5120,384]{2,1,0:T(8,128)(2,1)S(1)}, bf16[1,5120,384]{2,1,0:T(8,128)(2,1)}, u32[]{:S(2)}) copy-start(bf16[1,5120,384]{2,1,0:T(8,128)(2,1)} %param.17) | copy-start | bytes 11796484
  330.2 15.3 %copy-start.1 = (s32[2048]{0:T(1024)S(1)}, s32[2048]{0:T(1024)}, u32[]{:S(2)}) copy-start(s32[2048]{0:T(1024)} %param.19) | copy-start | bytes 24580
Sparse Core Ops, SparseCore 0:
  12.5 50.2 all-gather.5
  65.3 45.4 all-gather.7
  112.5 208.4 all-gather.11
  444.3 130.0 all-gather.9
where the time goes:
time: 597 us; the launch traced here: 596 us
  waiting for transfers between devices  429 us (72%)
  matrix products  115 us (19%)
  other arithmetic  17.4 us (3%)
  local copies, waits for them, and re-layouts  13.8 us (2%)
  between operations  13.2 us (2%)
  loops' own time  7.77 us (1%)
    all_gather x1, waiting for transfers between devices, body(): piece = lax.all_gather(layer_rows, 'ctx', axis=0, tiled=True)  208 us
    all_gather x1, waiting for transfers between devices, body(): lax.all_gather(context, 'ctx', axis=1, tiled=True)  130 us
    sub x4, matrix products, attend(): expo = jnp.where(visible[None], jnp.exp(scores - top), 0.0)  47.4 us
    all_gather x1, waiting for transfers between devices, body(): lax.all_gather(own_keys, 'section', axis=0, tiled=True)  45.9 us
    all_gather x1, waiting for transfers between devices, body(): lax.all_gather(own_values, 'section', axis=0, tiled=True)  44.6 us
    dot_general x4, matrix products, attend(): jnp.einsum('hqk,khd->qhd', weights, value_heads, preferred_element_type=j...  29.1 us
    dot_general x1, matrix products, body(): jnp.dot(lax.all_gather(context, 'ctx', axis=1, tiled=True), w_o, preferre...  15.5 us
    dot_general x1, matrix products, body(): jnp.dot(normalize(piece, gain), w_q, preferred_element_type=jnp.float32)  15.3 us
  transfers between devices with their start and end apart: 4, of which 4 were waited for; matrix products, arithmetic and copies ran while one was open for 2% of the time, Pallas kernels for 0%

commit v1 on v0

--- a/solution.py
+++ b/solution.py
@@ -28,7 +28,10 @@
     own_values = jnp.dot(kv_in, w_value, preferred_element_type=jnp.float32).astype(jnp.bfloat16)
     keys, values = (
         lax.all_gather(own_keys, "section", axis=0, tiled=True),
-        lax.all_gather(own_values, "section", axis=0, tiled=True),
+        jnp.concatenate(
+            lax.all_to_all(jnp.stack([own_values] * lax.axis_size("section")), "section", 0, 0),
+            axis=0,
+        ),
     )
     piece = lax.all_gather(layer_rows, "ctx", axis=0, tiled=True)
     queries_part = jnp.dot(normalize(piece, gain), w_q, preferred_element_type=jnp.float32).astype(

time: 597 us -> 555 us (0.930)
  waiting for transfers between devices: 429 us -> 377 us
  starting transfers between devices: 0.12 us -> 8.53 us
    all_gather x1 -> x0, waiting for transfers between devices: 44.6 us -> none  [body(): lax.all_gather(own_values, 'section', axis=0, tiled=True)]
    all_gather x1, waiting for transfers between devices: 45.9 us -> 15 us  [body(): lax.all_gather(own_keys, 'section', axis=0, tiled=True)]
    all_to_all x0 -> x1, waiting for transfers between devices: none -> 24.4 us  [body(): lax.all_to_all(jnp.stack([own_values] * lax.axis_size('section')), 'secti...]
    all_to_all x0 -> x1, starting transfers between devices: none -> 8.45 us  [body(): lax.all_to_all(jnp.stack([own_values] * lax.axis_size('section')), 'secti...]
where the time goes in v1:
time: 555 us; the launch traced here: 554 us
  waiting for transfers between devices  377 us (68%)
  matrix products  114 us (21%)
  other arithmetic  17.3 us (3%)
  local copies, waits for them, and re-layouts  16 us (3%)
  between operations  13.2 us (2%)
  starting transfers between devices  8.53 us (2%)
  loops' own time  7.69 us (1%)
    all_gather x1, waiting for transfers between devices, body(): piece = lax.all_gather(layer_rows, 'ctx', axis=0, tiled=True)  207 us
    all_gather x1, waiting for transfers between devices, body(): lax.all_gather(context, 'ctx', axis=1, tiled=True)  130 us
    sub x4, matrix products, attend(): expo = jnp.where(visible[None], jnp.exp(scores - top), 0.0)  47.4 us
    dot_general x4, matrix products, attend(): jnp.einsum('hqk,khd->qhd', weights, value_heads, preferred_element_type=j...  29.1 us
    all_to_all x1, waiting for transfers between devices, body(): lax.all_to_all(jnp.stack([own_values] * lax.axis_size('section')), 'secti...  24.4 us
    dot_general x1, matrix products, body(): jnp.dot(lax.all_gather(context, 'ctx', axis=1, tiled=True), w_o, preferre...  15.5 us
    dot_general x1, matrix products, body(): jnp.dot(normalize(piece, gain), w_q, preferred_element_type=jnp.float32)  15.3 us
    all_gather x1, waiting for transfers between devices, body(): lax.all_gather(own_keys, 'section', axis=0, tiled=True)  15 us
  transfers between devices with their start and end apart: 4, of which 4 were waited for; matrix products, arithmetic and copies ran while one was open for 2% of the time, Pallas kernels for 0%

profile of v1, /device:TPU:1, one launch (start us, length us, event | category | flops | bytes accessed | tf_op | source)
XLA Modules:
  0.0 554.4 jit_solution(7667474704015748915)
XLA Ops:
  6.5 1.6 fusion.36
  8.2 4.2 convolution_convert_fusion.1
  13.2 3.0 convolution_convert_fusion
  16.3 1.5 stack.2
  17.8 8.4 %all-to-all-start = ((bf16[16,128,384]{1,2,0:T(8,128)(2,1)}), bf16[16,128,384]{1,2,0:T(8,128)(2,1)S(1)}, u32[]{:S(2)}, u32[]{:S(2)}) async-start(bf16[16,128,384]{1,2,0:T(8,128)(2,1)} %stack.2), calls=%async_computation | async-start | bytes 3145728 | tf_op jit(solution)/shard_map/all_to_all | solution.py:32
  26.3 24.4 %all-to-all-done = bf16[16,128,384]{1,2,0:T(8,128)(2,1)S(1)} async-done(((bf16[16,128,384]{1,2,0:T(8,128)(2,1)}), bf16[16,128,384]{1,2,0:T(8,128)(2,1)S(1)}, u32[]{:S(2)}, u32[]{:S(2)}) %all-to-all-start) | async-done | bytes 1572896 | tf_op jit(solution)/shard_map/all_to_all | solution.py:32
  50.8 1.0 copy.27
  51.8 2.1 reshape_reshape.3
  53.9 15.0 %all-gather.5.cloned.1.call-done = bf16[2048,384]{1,0:T(8,128)(2,1)} async-done(((bf16[128,384]{1,0:T(8,128)(2,1)}), bf16[2048,384]{1,0:T(8,128)(2,1)}) %all-gather.5.cloned.1.call-update) | async-done | bytes 1572880 | tf_op jit(solution)/shard_map/all_gather | solution.py:30
  68.8 1.7 copy.25
  70.5 1.6 copy.29
  72.1 206.8 %all-gather.9.cloned.1.call-done = bf16[1,2048,5120]{2,1,0:T(8,128)(2,1)} async-done(((bf16[1,256,5120]{2,1,0:T(8,128)(2,1)}), bf16[1,2048,5120]{2,1,0:T(8,128)(2,1)}) %all-gather.9.cloned.1.call-update) | async-done | bytes 20971536 | tf_op jit(solution)/shard_map/all_gather | solution.py:36
  279.0 9.1 %fusion.14 = f32[2048]{0:T(1024)S(1)} fusion(bf16[1,2048,5120]{2,1,0:T(8,128)(2,1)} %all-gather.9.cloned.1.call-done), kind=kLoop, calls=%fused_computation.21 | loop fusion | flops 31455232 | bytes 20979712 | tf_op jit(solution)/shard_map/reduce_sum | solution.py:12
  288.2 15.3 %fusion.31 = bf16[2048,384]{1,0:T(8,128)(2,1)S(1)} fusion(bf16[1,5120,384]{2,1,0:T(8,128)(2,1)S(1)} %copy-done.2, bf16[1,2048,5120]{2,1,0:T(8,128)(2,1)} %all-gather.9.cloned.1.call-done, f32[5120]{0:T(1024)S(1)} %bitcast.60, f32[2048]{0:T(1024)S(1)} %add_rsqrt_fusion), kind=kOutput, calls=%fused_computation.36 | convolution fusion | flops 8095793152 | bytes 26505216 | tf_op jit(solution)/shard_map/dot_general | solution.py:37
  303.5 98.6 %while.11 = (s32[]{:T(128)}, bf16[4,512,384]{2,1,0:T(8,128)(2,1)}, s32[4]{0:T(128)S(1)}, s32[2048]{0:T(1024)S(1)}, bf16[2048,384]{1,0:T(8,128)(2,1)S(1)}, /*inde...) while((s32[]{:T(128)}, bf16[4,512,384]{2,1,0:T(8,128)(2,1)}, ...), condition=%wide.region_5.6_spmd.clone, body=%wide.region_2.5_spmd.clone.sunk | while | flops 1635977728 | bytes 34372256 | solution.py:70
  306.8 1.0 fusion.59
  308.1 11.8 %fusion.60 = (f32[3,512]{1,0:T(4,128)S(1)}, f32[3,512,2048]{2,1,0:T(8,128)}) fusion(pred[512,2048]{1,0:T(8,128)(4,1)S(1)} %fusion.59, bf16[512,3,128]{0,2,1:T(8,128)(2,1)S(1)} %bitcast.56, bf16[2048,3,128]{2,0,1:T(8,128)(2,1)} %get-tuple-element.180), kind=kOutput, calls=%fused_computation.45.clone.1 | convolution fusion | flops 821037056 | bytes 15603712 | tf_op jit(solution)/shard_map/while/body/eval_jaxpr/sub | solution.py:64
  320.0 7.3 %fusion.61 = bf16[3,512,128]{1,2,0:T(8,128)(2,1)S(1)} fusion(bf16[2048,3,128]{0,2,1:T(8,128)(2,1)} %get-tuple-element.181, f32[3,512,2048]{2,1,0:T(8,128)} %get-tuple-element.153, f32[3,512]{1,0:T(4,128)S(1)} %get-tuple-element.154), kind=kOutput, calls=%fused_computation.13.clone.1 | convolution fusion | flops 811794432 | bytes 14555136 | tf_op jit(solution)/shard_map/while/body/eval_jaxpr/hqk,khd->qhd/dot_general | solution.py:66
  327.5 0.8 constant_dynamic-update-slice_fusion.2
  331.4 1.0 fusion.59
  332.7 11.8 %fusion.60 = (f32[3,512]{1,0:T(4,128)S(1)}, f32[3,512,2048]{2,1,0:T(8,128)}) fusion(pred[512,2048]{1,0:T(8,128)(4,1)S(1)} %fusion.59, bf16[512,3,128]{0,2,1:T(8,128)(2,1)S(1)} %bitcast.56, bf16[2048,3,128]{2,0,1:T(8,128)(2,1)} %get-tuple-element.180), kind=kOutput, calls=%fused_computation.45.clone.1 | convolution fusion | flops 821037056 | bytes 15603712 | tf_op jit(solution)/shard_map/while/body/eval_jaxpr/sub | solution.py:64
  344.6 7.3 %fusion.61 = bf16[3,512,128]{1,2,0:T(8,128)(2,1)S(1)} fusion(bf16[2048,3,128]{0,2,1:T(8,128)(2,1)} %get-tuple-element.181, f32[3,512,2048]{2,1,0:T(8,128)} %get-tuple-element.153, f32[3,512]{1,0:T(4,128)S(1)} %get-tuple-element.154), kind=kOutput, calls=%fused_computation.13.clone.1 | convolution fusion | flops 811794432 | bytes 14555136 | tf_op jit(solution)/shard_map/while/body/eval_jaxpr/hqk,khd->qhd/dot_general | solution.py:66
  352.1 0.8 constant_dynamic-update-slice_fusion.2
  356.0 1.0 fusion.59
  357.3 11.8 %fusion.60 = (f32[3,512]{1,0:T(4,128)S(1)}, f32[3,512,2048]{2,1,0:T(8,128)}) fusion(pred[512,2048]{1,0:T(8,128)(4,1)S(1)} %fusion.59, bf16[512,3,128]{0,2,1:T(8,128)(2,1)S(1)} %bitcast.56, bf16[2048,3,128]{2,0,1:T(8,128)(2,1)} %get-tuple-element.180), kind=kOutput, calls=%fused_computation.45.clone.1 | convolution fusion | flops 821037056 | bytes 15603712 | tf_op jit(solution)/shard_map/while/body/eval_jaxpr/sub | solution.py:64
  369.2 7.3 %fusion.61 = bf16[3,512,128]{1,2,0:T(8,128)(2,1)S(1)} fusion(bf16[2048,3,128]{0,2,1:T(8,128)(2,1)} %get-tuple-element.181, f32[3,512,2048]{2,1,0:T(8,128)} %get-tuple-element.153, f32[3,512]{1,0:T(4,128)S(1)} %get-tuple-element.154), kind=kOutput, calls=%fused_computation.13.clone.1 | convolution fusion | flops 811794432 | bytes 14555136 | tf_op jit(solution)/shard_map/while/body/eval_jaxpr/hqk,khd->qhd/dot_general | solution.py:66
  380.6 1.0 fusion.59
  381.9 11.8 %fusion.60 = (f32[3,512]{1,0:T(4,128)S(1)}, f32[3,512,2048]{2,1,0:T(8,128)}) fusion(pred[512,2048]{1,0:T(8,128)(4,1)S(1)} %fusion.59, bf16[512,3,128]{0,2,1:T(8,128)(2,1)S(1)} %bitcast.56, bf16[2048,3,128]{2,0,1:T(8,128)(2,1)} %get-tuple-element.180), kind=kOutput, calls=%fused_computation.45.clone.1 | convolution fusion | flops 821037056 | bytes 15603712 | tf_op jit(solution)/shard_map/while/body/eval_jaxpr/sub | solution.py:64
  393.8 7.3 %fusion.61 = bf16[3,512,128]{1,2,0:T(8,128)(2,1)S(1)} fusion(bf16[2048,3,128]{0,2,1:T(8,128)(2,1)} %get-tuple-element.181, f32[3,512,2048]{2,1,0:T(8,128)} %get-tuple-element.153, f32[3,512]{1,0:T(4,128)S(1)} %get-tuple-element.154), kind=kOutput, calls=%fused_computation.13.clone.1 | convolution fusion | flops 811794432 | bytes 14555136 | tf_op jit(solution)/shard_map/while/body/eval_jaxpr/hqk,khd->qhd/dot_general | solution.py:66
  401.3 0.8 constant_dynamic-update-slice_fusion.2
  402.1 130.2 %all-gather.7.cloned.1.call-done = bf16[2048,3072]{1,0:T(8,128)(2,1)} async-done(((bf16[2048,384]{1,0:T(8,128)(2,1)}), bf16[2048,3072]{1,0:T(8,128)(2,1)}) %all-gather.7.cloned.1.call-update) | async-done | bytes 12582928 | tf_op jit(solution)/shard_map/all_gather | solution.py:72
  532.3 15.5 %fusion.28 = bf16[1,2048,640]{2,1,0:T(8,128)(2,1)} fusion(bf16[2048,3072]{1,0:T(8,128)(2,1)} %all-gather.7.cloned.1.call-done, bf16[1,3072,640]{2,1,0:T(8,128)(2,1)} %param.18, bf16[1,2048,5120]{2,1,0:T(8,128)(2,1)} %all-gather.9.cloned.1.call-done, s32[]{:T(128)S(6)} %select_n.14), kind=kOutput, calls=%fused_computation.35 | convolution fusion | flops 8056995840 | bytes 21757956 | tf_op jit(solution)/shard_map/dot_general | solution.py:71
  (46 shorter events, 9.0 us)
Async XLA Ops:
  6.5 62.3 %all-gather.5.cloned.1.call-start = ((), (), s32[]{:S(2)}) async-start(), calls=%async_computation.1 | async-start | bytes 1671168 | tf_op jit(solution)/shard_map/all_gather | solution.py:30
  8.2 5.0 copy-start
  8.2 5.0 copy-start.3
  12.4 266.6 %all-gather.9.cloned.1.call-start = ((), (), s32[]{:S(2)}) async-start(), calls=%async_computation.3 | async-start | bytes 23592960 | tf_op jit(solution)/shard_map/all_gather | solution.py:36
  17.8 32.9 %all-to-all-start = ((bf16[16,128,384]{1,2,0:T(8,128)(2,1)}), bf16[16,128,384]{1,2,0:T(8,128)(2,1)S(1)}, u32[]{:S(2)}, u32[]{:S(2)}) async-start(bf16[16,128,384]{1,2,0:T(8,128)(2,1)} %stack.2), calls=%async_computation | async-start | bytes 3145728 | tf_op jit(solution)/shard_map/all_to_all | solution.py:32
  26.3 506.1 %all-gather.7.cloned.1.call-start = ((), (), s32[]{:S(2)}) async-start(), calls=%async_computation.2 | async-start | bytes 14155776 | tf_op jit(solution)/shard_map/all_gather | solution.py:72
  72.1 216.0 %copy-start.4 = (f32[1,5120]{1,0:T(1,128)S(1)}, f32[1,5120]{1,0:T(1,128)}, u32[]{:S(2)}) copy-start(f32[1,5120]{1,0:T(1,128)} %param.14) | copy-start | bytes 61444
  279.0 9.2 %copy-start.2 = (bf16[1,5120,384]{2,1,0:T(8,128)(2,1)S(1)}, bf16[1,5120,384]{2,1,0:T(8,128)(2,1)}, u32[]{:S(2)}) copy-start(bf16[1,5120,384]{2,1,0:T(8,128)(2,1)} %param.17) | copy-start | bytes 11796484
  288.1 15.3 %copy-start.1 = (s32[2048]{0:T(1024)S(1)}, s32[2048]{0:T(1024)}, u32[]{:S(2)}) copy-start(s32[2048]{0:T(1024)} %param.19) | copy-start | bytes 24580
Sparse Core Ops, SparseCore 0:
  12.5 56.2 all-gather.4
  70.5 208.4 all-gather.8
  402.2 130.0 all-gather.6
